TPU v7x, 32 devices: a whole 2x2x4 slice. The times are simulated.
32 devices in a mesh: row: 8 (over y, x, core), col: 4 (over z).
Axes of the slice: x: 2, y: 2, z: 4, core: 2. Of those that a mesh axis runs over, the one named last changes fastest.
Arguments:
- covariance: float32 [2, 8, 512, 4, 4, 512], P(None, 'row', None, None, 'col'), as said below
- keep: int32 [2, 8, 4, 4], P(None, 'row', None, 'col'), may hold values from 0 to 1, as said below
Outputs:
- factor: float32 [2, 8, 512, 4, 4, 512], P(None, 'row', None, None, 'col')
Inputs may be any that keep to these rules, and one draw needn't show every extreme that they name: covariance is symmetric and positive definite. keep is 1 for every tile pair whose row and column tiles lie in the same diagonal super-tile of 4 tiles (i // 4 == j // 4).
All inputs are finite; a program needn't handle non-finite values.
Results may differ from a plain program's by a relative error of at most 0.0001.
Values sent between devices are 32-bit elements; how exact they have to be, the bound alone decides.
A program may use at most 128 MiB of HBM per device.

v0:
```python
import jax
import jax.numpy as jnp
from jax import lax
from jax.sharding import PartitionSpec as P


def from_root(block, axis, source):
    block = jnp.where(lax.axis_index(axis) == source, block, jnp.zeros_like(block))
    return lax.psum(block, axis)


def solve_rows(factor, column):
    count = column.shape[0]
    width = column.shape[1]
    stacked = jnp.transpose(column, (2, 0, 1)).reshape(width, count * width)
    solved = jax.scipy.linalg.solve_triangular(factor, stacked, lower=True)
    return jnp.transpose(solved.reshape(width, count, width), (1, 2, 0))


def finish(solved, factor, ids, step):
    return jnp.where(
        ids[:, None, None] > step,
        solved,
        jnp.where(ids[:, None, None] == step, factor[None], jnp.float32(0.0)),
    )


def shards(covariance, keep):
    row_count = lax.axis_size("row")
    col_count = lax.axis_size("col")
    row_here = lax.axis_index("row")
    col_here = lax.axis_index("col")
    tile_rows = covariance.shape[0]
    width = covariance.shape[2]
    tile_cols = covariance.shape[3]
    group = row_count // col_count
    tiles = covariance.reshape(tile_rows, width, tile_cols, width)
    row_ids = jnp.arange(tile_rows) * row_count + row_here
    col_ids = jnp.arange(tile_cols) * col_count + col_here
    live = (keep.reshape(tile_rows, tile_cols) > 0) & (row_ids[:, None] >= col_ids[None, :])
    tiles = jnp.where(live[:, None, :, None], tiles, jnp.float32(0.0))

    def spread_rows(block, step):
        return from_root(block, "col", step % col_count)

    def column_tiles(block):
        received = []
        for member in range(group):
            received.append(from_root(block, "row", col_here + member * col_count))
        stacked = jnp.stack(received, 1)
        return stacked.reshape(tile_rows * group, width, width)

    def factor_panel(column_block, step):
        local_diag = column_block[step // row_count]
        diag_tile = from_root(local_diag, "row", step % row_count)
        on_column = col_here == step % col_count
        factor = jnp.linalg.cholesky(diag_tile)
        row_panel = finish(solve_rows(factor, column_block), factor, row_ids, step)
        row_panel = jnp.where(on_column, row_panel, jnp.float32(0.0))
        row_panel = spread_rows(row_panel, step)
        col_panel = column_tiles(row_panel)
        return (row_panel, col_panel)

    def apply_update(block, row_panel, col_panel, step):
        product = jnp.einsum("arb,csb->arcs", row_panel, col_panel, precision=lax.Precision.HIGHEST)
        active = live & (row_ids > step)[:, None] & (col_ids > step)[None, :]
        updated = jnp.where(active[:, None, :, None], block - product, block)
        return jnp.where((col_ids == step)[None, None, :, None], row_panel[:, :, None, :], updated)

    first_rows, first_cols = factor_panel(tiles[:, :, 0, :], 0)
    tiles = apply_update(tiles, first_rows, first_cols, 0)
    second_rows, second_cols = factor_panel(tiles[:, :, 0, :], 1)
    tiles = apply_update(tiles, second_rows, second_cols, 1)
    return tiles.reshape(tile_rows, 1, width, tile_cols, 1, width)


def solution(mesh):
    placed = (P(None, "row", None, None, "col", None), P(None, "row", None, "col"))
    return jax.shard_map(
        shards,
        mesh=mesh,
        in_specs=placed,
        out_specs=P(None, "row", None, None, "col", None),
        check_vma=False,
    )
```

profile of v0, /device:TPU:25, one launch (start us, length us, event | category | flops | bytes accessed | tf_op | source)
XLA Modules:
  0.0 888.9 jit_solution(4985627599439522083)
XLA Ops:
  7.3 20.6 %copy.14 = f32[2,1,512,4,1,512]{2,5,3,0,4,1:T(8,128)} copy(f32[2,1,512,4,1,512]{5,4,3,2,1,0:T(1,128)} %param.5) | data formatting | bytes 16777216 | tf_op args[0]
  27.9 4.5 bitcast_select_fusion
  32.4 3.4 copy-done
  36.9 3.1 slice_bitcast_fusion.1
  40.1 1.9 copy.16
  42.0 51.5 %all-reduce.10.cloned.1.call-done = f32[512,512]{0,1:T(8,128)} async-done(((f32[512,512]{0,1:T(8,128)}), f32[512,512]{0,1:T(8,128)}) %all-reduce.10.cloned.1.call-update) | async-done | bytes 1048592 | tf_op jit(solution)/shard_map/psum | solution.py:9
  93.6 2.6 copy.15
  98.7 11.7 %cholesky.286 = f32[128,128]{1,0:T(8,128)S(1)} custom-call(f32[128,128]{1,0:T(8,128)S(1)} %cholesky.426), custom_call_target="Cholesky" | custom-call | tf_op jit(solution)/shard_map/jit(cholesky)/cholesky | solution.py:57
  110.4 9.8 %custom-call.27 = f32[1,128,128]{1,2,0:T(8,128)S(1)} custom-call(f32[1,128,128]{2,1,0:T(8,128)S(1)} %get-tuple-element.76), custom_call_target="InvertDiagBlocksLowerTriangular" | custom-call | tf_op jit(solution)/shard_map/jit(cholesky)/cholesky | solution.py:57
  122.9 11.7 %cholesky.305 = f32[128,128]{1,0:T(8,128)S(1)} custom-call(f32[128,128]{1,0:T(8,128)S(1)} %cholesky.430), custom_call_target="Cholesky" | custom-call | tf_op jit(solution)/shard_map/jit(cholesky)/cholesky | solution.py:57
  134.6 10.0 %custom-call.28 = f32[1,128,128]{1,2,0:T(8,128)S(1)} custom-call(f32[1,128,128]{2,1,0:T(8,128)S(1)} %get-tuple-element.73), custom_call_target="InvertDiagBlocksLowerTriangular" | custom-call | tf_op jit(solution)/shard_map/jit(cholesky)/cholesky | solution.py:57
  146.2 11.7 %cholesky.326 = f32[128,128]{1,0:T(8,128)S(1)} custom-call(f32[128,128]{1,0:T(8,128)S(1)} %cholesky.435), custom_call_target="Cholesky" | custom-call | tf_op jit(solution)/shard_map/jit(cholesky)/cholesky | solution.py:57
  158.6 9.8 %custom-call.29 = f32[1,128,128]{1,2,0:T(8,128)S(1)} custom-call(f32[1,128,128]{2,1,0:T(8,128)S(1)} %get-tuple-element.70), custom_call_target="InvertDiagBlocksLowerTriangular" | custom-call | tf_op jit(solution)/shard_map/jit(cholesky)/cholesky | solution.py:57
  169.9 11.7 %cholesky.343 = f32[128,128]{1,0:T(8,128)S(1)} custom-call(f32[128,128]{1,0:T(8,128)S(1)} %convolution_subtract_fusion.9), custom_call_target="Cholesky" | custom-call | tf_op jit(solution)/shard_map/jit(cholesky)/cholesky | solution.py:57
  185.6 1.8 fusion.34
  187.4 11.7 %while.4 = (s32[]{:T(128)}, f32[512,512]{1,0:T(8,128)}, s32[4,2]{0,1:T(2,128)S(1)}, f32[4,128,128]{2,1,0:T(8,128)S(1)}, s32[]{:T(128)}) while((s32[]{:T(128)}, f32[512,512]{1,0:T(8,128)}, s32[4,2]{0,1:T(2,128)S(1)}, f32[4,128,128]{2,1,0:T(8,128)S(1)}, s32[]{:T(128)}) %tuple.58), condition=%wide.while_cond, body=%wide.while_body.sunk | while | flops 2 | bytes 131181 | solution.py:16
  188.1 2.3 bitcast_dynamic-update-slice_fusion.4
  191.0 2.3 bitcast_dynamic-update-slice_fusion.4
  194.0 2.3 bitcast_dynamic-update-slice_fusion.4
  196.9 2.2 bitcast_dynamic-update-slice_fusion.4
  199.1 39.3 %custom-call.30 = f32[4,128,128]{1,2,0:T(8,128)S(1)} custom-call(f32[4,128,128]{2,1,0:T(8,128)S(1)} %get-tuple-element.21), custom_call_target="InvertDiagBlocksLowerTriangular" | custom-call | tf_op jit(solution)/shard_map/jit(_solve_triangular)/triangular_solve | solution.py:16
  239.1 1.8 convolution_subtract_fusion.3
  241.6 2.8 convolution_subtract_fusion.1
  245.0 3.7 fusion.20
  251.0 2.0 copy.32
  253.0 1.8 select_select_fusion.1
  254.8 85.0 %all-reduce.12.cloned.1.call-done = f32[2,512,512]{2,1,0:T(8,128)} async-done(((f32[2,512,512]{2,1,0:T(8,128)}), f32[2,512,512]{2,1,0:T(8,128)}) %all-reduce.12.cloned.1.call-update) | async-done | bytes 2097168 | tf_op jit(solution)/shard_map/psum | solution.py:9
  339.8 4.3 select_bitcast_fusion.3
  344.3 2.4 copy.18
  346.7 79.4 %all-reduce.20.cloned.1.call-done = (f32[2,1,512,512]{3,2,0,1:T(8,128)}, f32[2,1,512,512]{3,2,0,1:T(8,128)}) async-done(((f32[2,1,512,512]{3,2,0,1:T(8,128)}, f32[2,1,512,512]{3,2,0,1:T(8,128)}), (f32[2,1,512,512]{3,2,0,1:T(8,128)}, f32[2,1,512,512]{3,2,0,1:T(8,128)})) %all-reduce.20.cloned.1.call-update) | async-done | bytes 4194320 | tf_op jit(solution)/shard_map/psum | solution.py:9
  426.2 2.8 pad_maximum_fusion
  429.6 1.7 slice-done.1
  431.9 14.0 %fusion = f32[2,512,4,512]{1,3,2,0:T(8,128)S(1)} fusion(f32[2,512,4,512]{1,3,2,0:T(8,128)S(1)} %bitcast.156, f32[2,512,512]{1,2,0:T(8,128)S(1)} %copy.18, pred[4]{0:T(512)(128)(4,1)S(1)} %get-tuple-element.84, pred[2,4]{1,0:T(4,128)(4,1)S(1)} %bitcast.171, f32[4,512,512,1]{2,1,0,3:T(8,128)S(1)} %bitcast.159, f32[2,512,512]{2,1,0:T(8,128)S(1)} %copy-done.2), kind=kOutput, calls=%fused_computation.6 | convolution fusion | flops 12891193344 | bytes 25165836 | tf_op jit(solution)/shard_map/arb,csb->arcs/dot_general | solution.py:65
  445.9 3.4 copy-done.1
  450.5 3.1 slice_bitcast_fusion
  453.6 1.9 copy.22
  455.5 50.7 %all-reduce.14.cloned.1.call-done = f32[512,512]{0,1:T(8,128)} async-done(((f32[512,512]{0,1:T(8,128)}), f32[512,512]{0,1:T(8,128)}) %all-reduce.14.cloned.1.call-update) | async-done | bytes 1048592 | tf_op jit(solution)/shard_map/psum | solution.py:9
  506.2 2.6 copy.21
  511.3 11.7 %cholesky.358 = f32[128,128]{1,0:T(8,128)S(1)} custom-call(f32[128,128]{1,0:T(8,128)S(1)} %cholesky.439), custom_call_target="Cholesky" | custom-call | tf_op jit(solution)/shard_map/jit(cholesky)/cholesky | solution.py:57
  523.2 9.8 %custom-call.31 = f32[1,128,128]{1,2,0:T(8,128)S(1)} custom-call(f32[1,128,128]{2,1,0:T(8,128)S(1)} %get-tuple-element.66), custom_call_target="InvertDiagBlocksLowerTriangular" | custom-call | tf_op jit(solution)/shard_map/jit(cholesky)/cholesky | solution.py:57
  535.5 11.7 %cholesky.377 = f32[128,128]{1,0:T(8,128)S(1)} custom-call(f32[128,128]{1,0:T(8,128)S(1)} %cholesky.443), custom_call_target="Cholesky" | custom-call | tf_op jit(solution)/shard_map/jit(cholesky)/cholesky | solution.py:57
  548.6 10.2 %custom-call.32 = f32[1,128,128]{1,2,0:T(8,128)S(1)} custom-call(f32[1,128,128]{2,1,0:T(8,128)S(1)} %get-tuple-element.63), custom_call_target="InvertDiagBlocksLowerTriangular" | custom-call | tf_op jit(solution)/shard_map/jit(cholesky)/cholesky | solution.py:57
  560.4 11.7 %cholesky.398 = f32[128,128]{1,0:T(8,128)S(1)} custom-call(f32[128,128]{1,0:T(8,128)S(1)} %cholesky.448), custom_call_target="Cholesky" | custom-call | tf_op jit(solution)/shard_map/jit(cholesky)/cholesky | solution.py:57
  572.8 9.8 %custom-call.33 = f32[1,128,128]{1,2,0:T(8,128)S(1)} custom-call(f32[1,128,128]{2,1,0:T(8,128)S(1)} %get-tuple-element.60), custom_call_target="InvertDiagBlocksLowerTriangular" | custom-call | tf_op jit(solution)/shard_map/jit(cholesky)/cholesky | solution.py:57
  584.1 11.7 %cholesky.415 = f32[128,128]{1,0:T(8,128)S(1)} custom-call(f32[128,128]{1,0:T(8,128)S(1)} %convolution_subtract_fusion.8), custom_call_target="Cholesky" | custom-call | tf_op jit(solution)/shard_map/jit(cholesky)/cholesky | solution.py:57
  599.1 1.8 fusion.36
  600.9 11.7 %while.5 = (s32[]{:T(128)}, f32[512,512]{1,0:T(8,128)}, s32[4,2]{0,1:T(2,128)S(1)}, f32[4,128,128]{2,1,0:T(8,128)S(1)}, s32[]{:T(128)}) while((s32[]{:T(128)}, f32[512,512]{1,0:T(8,128)}, s32[4,2]{0,1:T(2,128)S(1)}, f32[4,128,128]{2,1,0:T(8,128)S(1)}, s32[]{:T(128)}) %tuple.78), condition=%wide.while_cond.clone, body=%wide.while_body.clone.sunk | while | flops 2 | bytes 131181 | solution.py:16
  601.6 2.3 bitcast_dynamic-update-slice_fusion.5
  604.5 2.3 bitcast_dynamic-update-slice_fusion.5
  607.5 2.3 bitcast_dynamic-update-slice_fusion.5
  610.4 2.2 bitcast_dynamic-update-slice_fusion.5
  612.6 39.3 %custom-call.34 = f32[4,128,128]{1,2,0:T(8,128)S(1)} custom-call(f32[4,128,128]{2,1,0:T(8,128)S(1)} %get-tuple-element.22), custom_call_target="InvertDiagBlocksLowerTriangular" | custom-call | tf_op jit(solution)/shard_map/jit(_solve_triangular)/triangular_solve | solution.py:16
  652.6 1.8 convolution_subtract_fusion.2
  655.1 2.8 convolution_subtract_fusion
  658.5 3.7 fusion.17
  664.4 2.0 copy.23
  666.5 1.8 select_select_fusion
  668.3 85.0 %all-reduce.16.cloned.1.call-done = f32[2,512,512]{2,1,0:T(8,128)} async-done(((f32[2,512,512]{2,1,0:T(8,128)}), f32[2,512,512]{2,1,0:T(8,128)}) %all-reduce.16.cloned.1.call-update) | async-done | bytes 2097168 | tf_op jit(solution)/shard_map/psum | solution.py:9
  753.3 4.3 select_bitcast_fusion.1
  757.7 2.1 copy.24
  759.8 79.8 %all-reduce.18.cloned.1.call-done = (f32[2,1,512,512]{3,2,0,1:T(8,128)}, f32[2,1,512,512]{3,2,0,1:T(8,128)}) async-done(((f32[2,1,512,512]{3,2,0,1:T(8,128)}, f32[2,1,512,512]{3,2,0,1:T(8,128)}), (f32[2,1,512,512]{3,2,0,1:T(8,128)}, f32[2,1,512,512]{3,2,0,1:T(8,128)})) %all-reduce.18.cloned.1.call-update) | async-done | bytes 4194320 | tf_op jit(solution)/shard_map/psum | solution.py:9
  839.6 2.8 pad_maximum_fusion.1
  845.4 15.9 %fusion.2 = f32[2,1,512,4,1,512]{2,5,3,0,4,1:T(8,128)} fusion(f32[2,512,4,512]{1,3,2,0:T(8,128)S(1)} %bitcast.158, f32[2,512,512]{1,2,0:T(8,128)S(1)} %copy.24, pred[4]{0:T(512)(128)(4,1)S(1)} %broadcast_compare_fusion.7, pred[2,4]{1,0:T(4,128)(4,1)S(1)} %bitcast.172, f32[4,512,512,1]{2,1,0,3:T(8,128)S(1)} %bitcast.160, f32[2,512,512]{2,1,0:T(8,128)S(1)} %copy-done.3), kind=kOutput, calls=%fused_computation.8 | convolution fusion | flops 12891193344 | bytes 25165836 | tf_op jit(solution)/shard_map/arb,csb->arcs/dot_general | solution.py:65
  861.3 20.5 %copy.27 = f32[2,1,512,4,1,512]{5,4,3,2,1,0:T(1,128)} copy(f32[2,1,512,4,1,512]{2,5,3,0,4,1:T(8,128)} %fusion.2) | data formatting | bytes 16777216 | tf_op jit(solution)/shard_map/reshape | solution.py:74
  (123 shorter events, 42.4 us)
Async XLA Ops:
  6.5 87.0 %all-reduce.10.cloned.1.call-start = ((), (), s32[]{:S(2)}) async-start(), calls=%async_computation | async-start | bytes 2097152 | tf_op jit(solution)/shard_map/psum | solution.py:9
  32.4 3.4 copy-start
  36.9 302.9 %all-reduce.12.cloned.1.call-start = ((), (), s32[]{:S(2)}) async-start(), calls=%async_computation.1 | async-start | bytes 4194304 | tf_op jit(solution)/shard_map/psum | solution.py:9
  93.6 2.6 copy-start.4
  97.7 1.0 copy-start.9
  251.0 2.0 copy-start.7
  254.8 171.4 %all-reduce.20.cloned.1.call-start = ((), (), s32[]{:S(2)}) async-start(), calls=%async_computation.5 | async-start | bytes 8388608 | tf_op jit(solution)/shard_map/psum | solution.py:9
  344.2 162.1 %all-reduce.14.cloned.1.call-start = ((), (), s32[]{:S(2)}) async-start(), calls=%async_computation.2 | async-start | bytes 2097152 | tf_op jit(solution)/shard_map/psum | solution.py:9
  426.2 3.4 slice-start
  429.0 2.3 slice-start.1
  429.0 2.9 copy-start.2
  445.9 3.4 copy-start.1
  450.4 302.9 %all-reduce.16.cloned.1.call-start = ((), (), s32[]{:S(2)}) async-start(), calls=%async_computation.3 | async-start | bytes 4194304 | tf_op jit(solution)/shard_map/psum | solution.py:9
  506.2 2.6 copy-start.5
  510.3 1.0 copy-start.8
  664.4 2.0 copy-start.6
  668.2 171.4 %all-reduce.18.cloned.1.call-start = ((), (), s32[]{:S(2)}) async-start(), calls=%async_computation.4 | async-start | bytes 8388608 | tf_op jit(solution)/shard_map/psum | solution.py:9
  839.6 3.4 slice-start.2
  842.5 2.3 slice-start.3
  842.5 2.9 copy-start.3
Sparse Core Ops, SparseCore 0:
  37.0 56.5 all-reduce.9
  254.9 84.8 all-reduce.11
  344.3 81.8 all-reduce.19
  450.5 55.6 all-reduce.13
  668.4 84.8 all-reduce.15
  757.8 81.8 all-reduce.17
where the time goes:
time: 903 us; the launch traced here: 889 us
  waiting for transfers between devices  432 us (48%)
  other arithmetic  272 us (30%)
  local copies, waits for them, and re-layouts  103 us (11%)
  matrix products  62.5 us (7%)
  between operations  19.5 us (2%)
    psum x6, waiting for transfers between devices, from_root(): return lax.psum(block, axis)  431 us
    another operation x29, other arithmetic, factor_panel(): factor = jnp.linalg.cholesky(diag_tile)  158 us
    another operation x7, other arithmetic, solve_rows(): solved = jax.scipy.linalg.solve_triangular(factor, stacked, lower=True)  85.4 us
    unnamed x32, local copies, waits for them, and re-layouts  34.3 us
    dot_general x2, matrix products, apply_update(): jnp.einsum('arb,csb->arcs', row_panel, col_panel, precision=lax.Precision...  29.9 us
    another operation x28, local copies, waits for them, and re-layouts, solve_rows(): solved = jax.scipy.linalg.solve_triangular(factor, stacked, lower=True)  25.3 us
    another operation x14, matrix products, solve_rows(): solved = jax.scipy.linalg.solve_triangular(factor, stacked, lower=True)  21.7 us
    reshape x1, local copies, waits for them, and re-layouts, shards(): return tiles.reshape(tile_rows, 1, width, tile_cols, 1, width)  20.5 us
  transfers between devices with their start and end apart: 6, of which 6 were waited for; matrix products, arithmetic and copies ran while one was open for 2% of the time, Pallas kernels for 0%

commit v1 on v0

v1 whole, which is shorter than its diff:
```python
import functools

import jax
import jax.numpy as jnp
from jax import lax
from jax.experimental import pallas as pl
from jax.experimental.pallas import tpu as pltpu
from jax.sharding import PartitionSpec as P

HIGH = lax.Precision.HIGHEST
MESH = pl.DeviceIdType.MESH
PIECES = 2
STEPS = 2


def schedule(group, tile_rows, bits):
    chain = [(a, k, h) for a in range(tile_rows) for h in range(PIECES) for k in range(STEPS)]
    tree = []
    events = []
    for n, (a, k, h) in enumerate(chain):
        events.append((n, 0, n, 0))
        found = []
        if a == 0 and k == 0:
            found.append(("fixed", 0, 0, a, k, h))
        if a == 0:
            found.append(("fixed", 1, 1 + k, a, k, h))
        for m in range(group):
            found.append(("own", m, 3 + (a * group + m) * STEPS + k, a, k, h))
        for item in found:
            for r in range(len(bits)):
                events.append((n + 1 + r, 1, len(tree), r))
            tree.append(item)
    return chain, tree, sorted(events)


def gather_kernel(row_count, col_count, tile_rows, x_ref, rows_ref, tree_ref, local_sem, zsend, zrecv, tsend, trecv):
    p = lax.axis_index("row")
    q = lax.axis_index("col")
    group = row_count // col_count
    bits = []
    bit = 2
    while bit < row_count:
        bits.append(bit)
        bit *= 2
    bits.append(1)
    chain, tree, events = schedule(group, tile_rows, bits)
    part = x_ref.shape[1] // PIECES

    barrier = pltpu.get_barrier_semaphore()
    for b in bits:
        pl.semaphore_signal(barrier, inc=1, device_id=(p ^ b, q), device_id_type=MESH)

    @pl.when(q > 0)
    def _():
        pl.semaphore_signal(barrier, inc=1, device_id=(p, q - 1), device_id_type=MESH)

    @pl.when(q < col_count - 1)
    def _():
        pl.semaphore_signal(barrier, inc=1, device_id=(p, q + 1), device_id_type=MESH)

    edges = (q > 0).astype(jnp.int32) + (q < col_count - 1).astype(jnp.int32)
    pl.semaphore_wait(barrier, len(bits) + edges)

    def chain_copy(n, way):
        a, k, h = chain[n]
        spot = pl.ds(h * part, part)
        return pltpu.make_async_remote_copy(
            src_ref=rows_ref.at[k, a, spot], dst_ref=rows_ref.at[k, a, spot],
            send_sem=zsend.at[n, (way + 1) // 2], recv_sem=zrecv.at[n],
            device_id=(p, q + way), device_id_type=MESH)

    def tree_copy(t, r):
        kind, source, slot, a, k, h = tree[t]
        spot = pl.ds(h * part, part)
        return pltpu.make_async_remote_copy(
            src_ref=tree_ref.at[slot, spot], dst_ref=tree_ref.at[slot, spot],
            send_sem=tsend.at[t, r], recv_sem=trecv.at[t],
            device_id=(p ^ bits[r], q), device_id_type=MESH)

    def local(src, dst):
        copy = pltpu.make_async_copy(src, dst, local_sem)
        copy.start()
        copy.wait()

    def relative(t):
        kind, source = tree[t][:2]
        return p ^ (source if kind == "fixed" else q + source * col_count)

    def sends(t, r):
        waiting = 0
        for b in bits[r:]:
            waiting |= b
        return (relative(t) & waiting) == 0

    def receives(t, r):
        later = 0
        for b in bits[r + 1:]:
            later |= b
        rel = relative(t)
        return ((rel & bits[r]) != 0) & ((rel & later) == 0)

    def up(k):
        return (q >= k) & (q < col_count - 1)

    def down(k):
        return (q <= k) & (q > 0)

    for k in range(STEPS):
        @pl.when(q == k)
        def _():
            local(x_ref, rows_ref.at[k])

    for when, what, n, r in events:
        if what == 0:
            k = chain[n][1]

            @pl.when(q != k)
            def _():
                chain_copy(n, 1).wait_recv()

            @pl.when(up(k))
            def _():
                chain_copy(n, 1).start()

            @pl.when(down(k))
            def _():
                chain_copy(n, -1).start()
        else:
            kind, source, slot, a, k, h = tree[n]
            spot = pl.ds(h * part, part)
            if r == 0:
                @pl.when(relative(n) == 0)
                def _():
                    local(rows_ref.at[k, a, spot], tree_ref.at[slot, spot])

            @pl.when(sends(n, r))
            def _():
                tree_copy(n, r).start()

            @pl.when(receives(n, r))
            def _():
                tree_copy(n, r).wait_recv()

    for n in range(len(chain)):
        k = chain[n][1]

        @pl.when(up(k))
        def _():
            chain_copy(n, 1).wait_send()

        @pl.when(down(k))
        def _():
            chain_copy(n, -1).wait_send()

    for t in range(len(tree)):
        for r in range(len(bits)):
            @pl.when(sends(t, r))
            def _():
                tree_copy(t, r).wait_send()


def gather(x, row_count, col_count):
    tile_rows, height, width = x.shape
    group = row_count // col_count
    slots = 3 + tile_rows * group * STEPS
    bits = row_count.bit_length() - 1
    chain, tree, _ = schedule(group, tile_rows, [0] * bits)
    anywhere = pl.BlockSpec(memory_space=pl.ANY)
    return pl.pallas_call(
        functools.partial(gather_kernel, row_count, col_count, tile_rows),
        out_shape=(
            jax.ShapeDtypeStruct((STEPS, tile_rows, height, width), jnp.float32),
            jax.ShapeDtypeStruct((slots, height, width), jnp.float32),
        ),
        in_specs=[anywhere],
        out_specs=(anywhere, anywhere),
        scratch_shapes=[
            pltpu.SemaphoreType.DMA,
            pltpu.SemaphoreType.DMA((len(chain), 2)),
            pltpu.SemaphoreType.DMA((len(chain),)),
            pltpu.SemaphoreType.DMA((len(tree), bits)),
            pltpu.SemaphoreType.DMA((len(tree),)),
        ],
        compiler_params=pltpu.CompilerParams(collective_id=0, has_side_effects=True),
    )(x)


def mm(a, b):
    return jnp.matmul(a, b, precision=HIGH)


def factor_block(block):
    lower = jnp.linalg.cholesky(block)
    eye = jnp.eye(block.shape[0], dtype=jnp.float32)
    return lower, lax.linalg.triangular_solve(lower, eye, left_side=True, lower=True)


def factor_and_inverse(block):
    width = block.shape[0]
    if width <= 128:
        return factor_block(block)
    half = width // 2
    l00, i00 = factor_and_inverse(block[:half, :half])
    l10 = mm(block[half:, :half], i00.T)
    l11, i11 = factor_and_inverse(block[half:, half:] - mm(l10, l10.T))
    i10 = -mm(i11, mm(l10, i00))
    zero = jnp.zeros((half, half), jnp.float32)
    return jnp.block([[l00, zero], [l10, l11]]), jnp.block([[i00, zero], [i10, i11]])


def shards(covariance, keep):
    row_count = lax.axis_size("row")
    col_count = lax.axis_size("col")
    row_here = lax.axis_index("row")
    col_here = lax.axis_index("col")
    tile_rows = covariance.shape[0]
    width = covariance.shape[2]
    tile_cols = covariance.shape[3]
    tiles = covariance.reshape(tile_rows, width, tile_cols, width)
    row_ids = jnp.arange(tile_rows) * row_count + row_here
    col_ids = jnp.arange(tile_cols) * col_count + col_here
    live = (keep.reshape(tile_rows, tile_cols) > 0) & (row_ids[:, None] >= col_ids[None, :])
    first = jnp.where(live[:, 0, None, None], covariance[:, 0, :, 0, 0, :], jnp.float32(0.0))
    marks = jnp.broadcast_to(live[:, 0, None, None].astype(jnp.float32), (tile_rows, 8 * PIECES, width))
    rows, tree = gather(jnp.concatenate([first, marks], 1), row_count, col_count)

    row_marks = rows[1, :, width, :1]
    row_tiles = rows[:, :, :width, :]
    cols = tree[3:].reshape(tile_cols, STEPS, -1, width)
    col_marks = cols[:, 1, width, :1]
    col_tiles = cols[:, :, :width, :]
    diag = tree[:3, :width, :]

    def symmetric(block):
        return (block + block.T) * 0.5

    low0, inv0 = factor_and_inverse(symmetric(diag[0]))
    below = mm(diag[1], inv0.T)
    low1, inv1 = factor_and_inverse(symmetric(diag[2] - mm(below, below.T)))

    def panels(first_tiles, second_tiles, marks, ids):
        ids = ids[:, None, None]
        one = mm(first_tiles, inv0.T)
        one = jnp.where(ids > 0, one, jnp.float32(0.0))
        two = second_tiles - mm(one, below.T) * marks[:, :, None]
        two = jnp.where(ids > 1, mm(two, inv1.T), jnp.float32(0.0))
        return one, two

    row_one, row_two = panels(row_tiles[0], row_tiles[1], row_marks, row_ids)
    col_one, col_two = panels(col_tiles[:, 0], col_tiles[:, 1], col_marks, col_ids)
    row_all = jnp.concatenate([row_one, row_two], 2)
    col_all = jnp.concatenate([col_one, col_two], 2)
    product = jnp.einsum("arb,csb->arcs", row_all, col_all, precision=HIGH)
    tiles = jnp.where(live[:, None, :, None], tiles - product, jnp.float32(0.0))
    ids = row_ids[:, None, None]
    done_one = jnp.where(ids == 0, low0[None], row_one)
    done_two = jnp.where(ids == 1, low1[None], row_two)
    column = jnp.where(col_here == 0, done_one, done_two)
    place = (col_ids < STEPS)[None, None, :, None]
    tiles = jnp.where(place, column[:, :, None, :], tiles)
    return tiles.reshape(tile_rows, 1, width, tile_cols, 1, width)


def solution(mesh):
    placed = (P(None, "row", None, None, "col", None), P(None, "row", None, "col"))
    return jax.shard_map(
        shards,
        mesh=mesh,
        in_specs=placed,
        out_specs=P(None, "row", None, None, "col", None),
        check_vma=False,
    )
```

time: 903 us -> 884 us (0.979)
  Pallas kernels: 0 us -> 553 us
  waiting for transfers between devices: 432 us -> 0 us
  other arithmetic: 272 us -> 194 us
  local copies, waits for them, and re-layouts: 103 us -> 29.4 us
  matrix products: 62.5 us -> 96.2 us
  between operations: 19.5 us -> 1.45 us
    pallas_call x0 -> x1, Pallas kernels: none -> 553 us  [gather(): pl.pallas_call(functools.partial(gather_kernel, row_count, col_count, til...]
    psum x6 -> x0, waiting for transfers between devices: 431 us -> none  [from_root(): return lax.psum(block, axis)]
    another operation x40, other arithmetic: 258 us -> 187 us  [the longest x24 100 us: factor_block(): lower = jnp.linalg.cholesky(block)]
    dot_general x2 -> x33, matrix products: 29.9 us -> 94 us  [the longest x32 61.9 us: mm(): return jnp.matmul(a, b, precision=HIGH)]
    another operation x26 -> x8, matrix products: 32.6 us -> 2.2 us  [factor_block(): lax.linalg.triangular_solve(lower, eye, left_side=True, lower=True)]
    unnamed x32 -> x50, local copies, waits for them, and re-layouts: 34.3 us -> 4.45 us
    another operation x38 -> x4, local copies, waits for them, and re-layouts: 26.5 us -> 0.35 us  [factor_block(): lax.linalg.triangular_solve(lower, eye, left_side=True, lower=True)]
    transpose x4 -> x0, local copies, waits for them, and re-layouts: 10.1 us -> none  [solve_rows(): stacked = jnp.transpose(column, (2, 0, 1)).reshape(width, count * width)]
  transfers between devices with their start and end apart: 6 -> 0, of which waited for: 6 -> 0; matrix products, arithmetic and copies ran while one was open for 2% -> 0% of each run, Pallas kernels for 0% -> 0%
where the time goes in v1:
time: 884 us; the launch traced here: 874 us
  Pallas kernels  553 us (63%)
  other arithmetic  194 us (22%)
  matrix products  96.2 us (11%)
  local copies, waits for them, and re-layouts  29.4 us (3%)
    pallas_call x1, Pallas kernels, gather(): pl.pallas_call(functools.partial(gather_kernel, row_count, col_count, til...  553 us
    another operation x24, other arithmetic, factor_block(): lower = jnp.linalg.cholesky(block)  100 us
    another operation x16, other arithmetic, factor_block(): lax.linalg.triangular_solve(lower, eye, left_side=True, lower=True)  86.6 us
    dot_general x32, matrix products, mm(): return jnp.matmul(a, b, precision=HIGH)  61.9 us
    dot_general x1, matrix products, shards(): product = jnp.einsum('arb,csb->arcs', row_all, col_all, precision=HIGH)  32.1 us

profile of v1, /device:TPU:25, one launch (start us, length us, event | category | flops | bytes accessed | tf_op | source)
XLA Modules:
  0.0 874.3 jit_solution(11093627586163587748)
XLA Ops:
  0.1 0.9 compare_and_fusion
  2.0 1.5 pad_maximum_fusion.x_ref
  3.5 552.9 %shard_map.28 = (f32[2,2,528,512]{3,2,1,0:T(8,128)}, f32[11,528,512]{2,1,0:T(8,128)}) custom-call(f32[2,528,512]{2,1,0:T(8,128)} %pad_maximum_fusion.x_ref), custom_call_target="tpu_custom_call" | custom-call | tf_op jit(solution)/shard_map/pallas_call | solution.py:169
  556.4 0.8 slice_reduce_fusion.1
  557.2 1.3 slice_bitcast_fusion.5
  558.9 1.4 fusion.34
  560.5 11.7 %cholesky.134 = f32[128,128]{1,0:T(8,128)S(1)} custom-call(f32[128,128]{1,0:T(8,128)S(1)} %fusion.107), custom_call_target="Cholesky" | custom-call | tf_op jit(solution)/shard_map/jit(cholesky)/cholesky | solution.py:193
  572.2 0.6 compare_reduce_fusion.7
  572.9 0.7 select_bitcast_fusion.7
  573.5 9.8 %custom-call.12 = f32[1,128,128]{1,2,0:T(8,128)S(1)} custom-call(f32[1,128,128]{2,1,0:T(8,128)S(1)} %get-tuple-element.25), custom_call_target="InvertDiagBlocksLowerTriangular" | custom-call | tf_op jit(solution)/shard_map/triangular_solve/custom-call.0 | solution.py:195
  584.2 12.0 %cholesky.145 = f32[128,128]{1,0:T(8,128)S(1)} custom-call(f32[128,128]{1,0:T(8,128)S(1)} %fusion.105), custom_call_target="Cholesky" | custom-call | tf_op jit(solution)/shard_map/jit(cholesky)/cholesky | solution.py:193
  596.3 0.6 compare_reduce_fusion.6
  597.0 0.7 select_bitcast_fusion.6
  597.6 9.8 %custom-call.13 = f32[1,128,128]{1,2,0:T(8,128)S(1)} custom-call(f32[1,128,128]{2,1,0:T(8,128)S(1)} %get-tuple-element.23), custom_call_target="InvertDiagBlocksLowerTriangular" | custom-call | tf_op jit(solution)/shard_map/triangular_solve/custom-call.0 | solution.py:195
  608.5 0.7 select_maximum_fusion.7
  609.6 0.6 convolution_subtract_fusion.2
  610.3 11.7 %cholesky.156 = f32[128,128]{1,0:T(8,128)S(1)} custom-call(f32[128,128]{1,0:T(8,128)S(1)} %fusion.103), custom_call_target="Cholesky" | custom-call | tf_op jit(solution)/shard_map/jit(cholesky)/cholesky | solution.py:193
  622.1 0.6 compare_reduce_fusion.5
  622.7 1.3 select_bitcast_fusion.5
  624.0 9.8 %custom-call.14 = f32[1,128,128]{1,2,0:T(8,128)S(1)} custom-call(f32[1,128,128]{2,1,0:T(8,128)S(1)} %get-tuple-element.21), custom_call_target="InvertDiagBlocksLowerTriangular" | custom-call | tf_op jit(solution)/shard_map/triangular_solve/custom-call.0 | solution.py:195
  634.7 11.9 %cholesky.167 = f32[128,128]{1,0:T(8,128)S(1)} custom-call(f32[128,128]{1,0:T(8,128)S(1)} %fusion.101), custom_call_target="Cholesky" | custom-call | tf_op jit(solution)/shard_map/jit(cholesky)/cholesky | solution.py:193
  646.6 0.6 compare_reduce_fusion.4
  647.3 1.3 select_bitcast_fusion.4
  648.6 9.8 %custom-call.15 = f32[1,128,128]{1,2,0:T(8,128)S(1)} custom-call(f32[1,128,128]{2,1,0:T(8,128)S(1)} %get-tuple-element.19), custom_call_target="InvertDiagBlocksLowerTriangular" | custom-call | tf_op jit(solution)/shard_map/triangular_solve/custom-call.0 | solution.py:195
  659.3 0.7 copy.55
  660.1 0.6 fusion.117
  661.1 0.8 copy.56
  662.0 3.1 fusion.40
  665.0 3.1 convolution_subtract_fusion
  668.1 4.6 slice.133
  672.7 3.3 copy-done
  676.7 1.0 copy-done.1
  677.7 0.9 fusion.99
  678.6 11.9 %cholesky.178 = f32[128,128]{1,0:T(8,128)S(1)} custom-call(f32[128,128]{1,0:T(8,128)S(1)} %fusion.99), custom_call_target="Cholesky" | custom-call | tf_op jit(solution)/shard_map/jit(cholesky)/cholesky | solution.py:193
  690.5 0.7 compare_reduce_fusion.3
  691.2 0.6 select_bitcast_fusion.3
  691.8 9.8 %custom-call.16 = f32[1,128,128]{1,2,0:T(8,128)S(1)} custom-call(f32[1,128,128]{2,1,0:T(8,128)S(1)} %get-tuple-element.17), custom_call_target="InvertDiagBlocksLowerTriangular" | custom-call | tf_op jit(solution)/shard_map/triangular_solve/custom-call.0 | solution.py:195
  702.0 1.0 fusion.86
  703.0 1.1 convolution_subtract_fusion.4
  704.3 11.7 %cholesky.189 = f32[128,128]{1,0:T(8,128)S(1)} custom-call(f32[128,128]{1,0:T(8,128)S(1)} %fusion.97), custom_call_target="Cholesky" | custom-call | tf_op jit(solution)/shard_map/jit(cholesky)/cholesky | solution.py:193
  716.0 0.7 compare_reduce_fusion.2
  716.7 0.6 select_bitcast_fusion.2
  717.3 10.3 %custom-call.17 = f32[1,128,128]{1,2,0:T(8,128)S(1)} custom-call(f32[1,128,128]{2,1,0:T(8,128)S(1)} %get-tuple-element.15), custom_call_target="InvertDiagBlocksLowerTriangular" | custom-call | tf_op jit(solution)/shard_map/triangular_solve/custom-call.0 | solution.py:195
  728.7 1.3 fusion.54
  730.0 1.5 convolution_subtract_fusion.1
  731.7 11.7 %cholesky.200 = f32[128,128]{1,0:T(8,128)S(1)} custom-call(f32[128,128]{1,0:T(8,128)S(1)} %fusion.95), custom_call_target="Cholesky" | custom-call | tf_op jit(solution)/shard_map/jit(cholesky)/cholesky | solution.py:193
  743.4 0.6 compare_reduce_fusion.1
  744.1 1.3 select_bitcast_fusion.1
  745.4 9.8 %custom-call.18 = f32[1,128,128]{1,2,0:T(8,128)S(1)} custom-call(f32[1,128,128]{2,1,0:T(8,128)S(1)} %get-tuple-element.13), custom_call_target="InvertDiagBlocksLowerTriangular" | custom-call | tf_op jit(solution)/shard_map/triangular_solve/custom-call.0 | solution.py:195
  756.1 11.9 %cholesky.211 = f32[128,128]{1,0:T(8,128)S(1)} custom-call(f32[128,128]{1,0:T(8,128)S(1)} %fusion.93), custom_call_target="Cholesky" | custom-call | tf_op jit(solution)/shard_map/jit(cholesky)/cholesky | solution.py:193
  768.0 0.6 compare_reduce_fusion
  768.7 1.3 select_bitcast_fusion
  770.0 9.8 %custom-call.19 = f32[1,128,128]{1,2,0:T(8,128)S(1)} custom-call(f32[1,128,128]{2,1,0:T(8,128)S(1)} %get-tuple-element.11), custom_call_target="InvertDiagBlocksLowerTriangular" | custom-call | tf_op jit(solution)/shard_map/triangular_solve/custom-call.0 | solution.py:195
  780.7 0.7 copy.72
  782.5 0.8 copy.73
  783.3 1.4 fusion.30
  784.8 5.2 fusion.24
  790.0 3.5 fusion.37
  793.6 7.8 select_select_fusion
  801.4 6.8 fusion.13
  808.3 13.4 %fusion.35 = f32[4,512,512]{2,1,0:T(8,128)S(1)} fusion(f32[4,512,512]{1,2,0:T(8,128)S(1)} %fusion.13, f32[512,512]{1,0:T(8,128)S(1)} %fusion.40), kind=kOutput, calls=%fused_computation.62 | convolution fusion | flops 6442450944 | bytes 9437184 | tf_op jit(solution)/shard_map/dot_general | solution.py:189
  821.7 7.4 broadcast_select_fusion
  829.1 32.1 %fusion.5 = f32[2,1,512,4,1,512]{5,2,3,0,4,1:T(8,128)S(1)} fusion(f32[2,1,512,4,1,512]{5,4,3,2,1,0:T(1,128)S(1)} %bitcast.209, f32[2,512,512]{2,1,0:T(8,128)} %get-tuple-element.29, pred[4]{0:T(512)(128)(4,1)S(1)} %broadcast_compare_fusion.7, pred[2,4]{1,0:T(4,128)(4,1)S(1)} %bitcast.211, f32[4,512,512]{1,2,0:T(8,128)S(1)} %broadcast_select_fusion, ...), kind=kOutput, calls=%fused_computation.7 | convolution fusion | flops 25779240960 | bytes 31457292 | tf_op jit(solution)/shard_map/arb,csb->arcs/dot_general | solution.py:253
  861.2 12.7 %copy.82 = f32[2,1,512,4,1,512]{5,4,3,2,1,0:T(1,128)} copy(f32[2,1,512,4,1,512]{5,2,3,0,4,1:T(8,128)S(1)} %fusion.5) | data formatting | bytes 16777216 | tf_op jit(solution)/shard_map/reshape | solution.py:261
  (131 shorter events, 11.6 us)
Async XLA Ops:
  0.0 1.6 slice-start.5
  658.7 3.2 copy-start.17
  659.3 2.6 copy-start.15
  660.1 1.8 copy-start.13
  661.1 0.8 copy-start.10
  672.7 3.3 copy-start
  676.7 1.0 copy-start.1
  727.6 55.8 %copy-start.12 = (f32[256,256]{1,0:T(8,128)S(1)}, f32[256,256]{1,0:T(8,128)}, u32[]{:S(2)}) copy-start(f32[256,256]{1,0:T(8,128)} %select_maximum_fusion.7) | copy-start | bytes 786436
  744.1 40.7 %copy-start.11 = (f32[256,256]{1,0:T(8,128)S(1)}, f32[256,256]{1,0:T(8,128)}, u32[]{:S(2)}) copy-start(f32[256,256]{1,0:T(8,128)} %copy-done.10) | copy-start | bytes 786436
  744.1 40.7 %copy-start.14 = (f32[256,256]{1,0:T(8,128)S(1)}, f32[256,256]{1,0:T(8,128)}, u32[]{:S(2)}) copy-start(f32[256,256]{1,0:T(8,128)} %copy-done.13) | copy-start | bytes 786436
  780.1 13.4 %copy-start.8 = (f32[128,128]{1,0:T(8,128)}, f32[128,128]{1,0:T(8,128)S(1)}, u32[]{:S(2)}) copy-start(f32[128,128]{1,0:T(8,128)S(1)} %copy.75) | copy-start | bytes 196612
  781.5 12.1 %copy-start.6 = (f32[128,256]{1,0:T(8,128)}, f32[128,256]{1,0:T(8,128)S(1)}, u32[]{:S(2)}) copy-start(f32[128,256]{1,0:T(8,128)S(1)} %concatenate.155) | copy-start | bytes 393220
  781.5 12.0 %copy-start.2 = (f32[256,256]{1,0:T(8,128)}, f32[256,256]{1,0:T(8,128)S(1)}, u32[]{:S(2)}) copy-start(f32[256,256]{1,0:T(8,128)S(1)} %select_maximum_fusion.4) | copy-start | bytes 786436
  782.5 11.1 %copy-start.4 = (f32[256,256]{1,0:T(8,128)}, f32[256,256]{1,0:T(8,128)S(1)}, u32[]{:S(2)}) copy-start(f32[256,256]{1,0:T(8,128)S(1)} %convolution_negate_fusion) | copy-start | bytes 786436
  784.8 16.6 %slice-start = ((s8[8650752]{0:T(1024)(128)(4,1)}), s8[4194304]{0:T(1024)(128)(4,1)S(1)}, s32[]{:S(2)}) async-start(s8[8650752]{0:T(1024)(128)(4,1)} %bitcast.204), calls=%async_computation | async-start | bytes 8388608
  790.0 11.4 %slice-start.1 = ((s8[8650752]{0:T(1024)(128)(4,1)}), s8[4194304]{0:T(1024)(128)(4,1)S(1)}, s32[]{:S(2)}) async-start(s8[8650752]{0:T(1024)(128)(4,1)} %bitcast.204), calls=%async_computation.1 | async-start | bytes 8388608
  793.6 7.8 slice-start.2
  793.6 7.8 copy-start.16
  793.6 7.8 copy-start.18
  808.3 13.4 %copy-start.3 = (f32[256,256]{1,0:T(8,128)S(1)}, f32[256,256]{1,0:T(8,128)}, u32[]{:S(2)}) copy-start(f32[256,256]{1,0:T(8,128)} %copy-done.2) | copy-start | bytes 786436
  808.3 13.4 %copy-start.5 = (f32[256,256]{1,0:T(8,128)S(1)}, f32[256,256]{1,0:T(8,128)}, u32[]{:S(2)}) copy-start(f32[256,256]{1,0:T(8,128)} %copy-done.4) | copy-start | bytes 786436
  808.3 13.4 %copy-start.7 = (f32[128,256]{1,0:T(8,128)S(1)}, f32[128,256]{1,0:T(8,128)}, u32[]{:S(2)}) copy-start(f32[128,256]{1,0:T(8,128)} %copy-done.6) | copy-start | bytes 393220
  808.3 13.4 %copy-start.9 = (f32[128,128]{1,0:T(8,128)S(1)}, f32[128,128]{1,0:T(8,128)}, u32[]{:S(2)}) copy-start(f32[128,128]{1,0:T(8,128)} %copy-done.8) | copy-start | bytes 196612
  808.3 20.8 %slice-start.3 = ((s8[8388608]{0:T(1024)(128)(4,1)}), s8[4194304]{0:T(1024)(128)(4,1)S(1)}, s32[]{:S(2)}) async-start(s8[8388608]{0:T(1024)(128)(4,1)} %bitcast.208), calls=%async_computation.3 | async-start | bytes 8388608
  821.7 7.4 slice-start.4

commit v2 on v0

--- a/solution.py
+++ b/solution.py
@@ -2,6 +2,8 @@
 import jax.numpy as jnp
 from jax import lax
 from jax.sharding import PartitionSpec as P
+
+HIGH = lax.Precision.HIGHEST
 
 
 def from_root(block, axis, source):
@@ -9,12 +11,27 @@
     return lax.psum(block, axis)
 
 
-def solve_rows(factor, column):
-    count = column.shape[0]
-    width = column.shape[1]
-    stacked = jnp.transpose(column, (2, 0, 1)).reshape(width, count * width)
-    solved = jax.scipy.linalg.solve_triangular(factor, stacked, lower=True)
-    return jnp.transpose(solved.reshape(width, count, width), (1, 2, 0))
+def mm(a, b):
+    return jnp.matmul(a, b, precision=HIGH)
+
+
+def factor_block(block):
+    lower = jnp.linalg.cholesky(block)
+    eye = jnp.eye(block.shape[0], dtype=jnp.float32)
+    return lower, lax.linalg.triangular_solve(lower, eye, left_side=True, lower=True)
+
+
+def factor_and_inverse(block):
+    width = block.shape[0]
+    if width <= 128:
+        return factor_block(block)
+    half = width // 2
+    l00, i00 = factor_and_inverse(block[:half, :half])
+    l10 = mm(block[half:, :half], i00.T)
+    l11, i11 = factor_and_inverse(block[half:, half:] - mm(l10, l10.T))
+    i10 = -mm(i11, mm(l10, i00))
+    zero = jnp.zeros((half, half), jnp.float32)
+    return jnp.block([[l00, zero], [l10, l11]]), jnp.block([[i00, zero], [i10, i11]])
 
 
 def finish(solved, factor, ids, step):
@@ -54,8 +71,8 @@
         local_diag = column_block[step // row_count]
         diag_tile = from_root(local_diag, "row", step % row_count)
         on_column = col_here == step % col_count
-        factor = jnp.linalg.cholesky(diag_tile)
-        row_panel = finish(solve_rows(factor, column_block), factor, row_ids, step)
+        factor, inverse = factor_and_inverse((diag_tile + diag_tile.T) * 0.5)
+        row_panel = finish(mm(column_block, inverse.T), factor, row_ids, step)
         row_panel = jnp.where(on_column, row_panel, jnp.float32(0.0))
         row_panel = spread_rows(row_panel, step)
         col_panel = column_tiles(row_panel)

time: 903 us -> 758 us (0.84)
  local copies, waits for them, and re-layouts: 103 us -> 30.7 us
  other arithmetic: 272 us -> 209 us
  waiting for transfers between devices: 432 us -> 445 us
  matrix products: 62.5 us -> 51.4 us
    another operation x36 -> x40, other arithmetic: 244 us -> 185 us  [the longest x24 100 us: factor_block(): lower = jnp.linalg.cholesky(block)]
    another operation x26 -> x8, matrix products: 32.6 us -> 2.2 us  [factor_block(): lax.linalg.triangular_solve(lower, eye, left_side=True, lower=True)]
    another operation x36 -> x4, local copies, waits for them, and re-layouts: 25.6 us -> 0.35 us  [factor_block(): lax.linalg.triangular_solve(lower, eye, left_side=True, lower=True)]
    unnamed x32 -> x23, local copies, waits for them, and re-layouts: 34.3 us -> 11.8 us
    dot_general x0 -> x26, matrix products: none -> 21.2 us  [mm(): return jnp.matmul(a, b, precision=HIGH)]
    psum x6, waiting for transfers between devices: 431 us -> 445 us  [from_root(): return lax.psum(block, axis)]
    transpose x4 -> x0, local copies, waits for them, and re-layouts: 10.1 us -> none  [solve_rows(): stacked = jnp.transpose(column, (2, 0, 1)).reshape(width, count * width)]
  transfers between devices with their start and end apart: 6 -> 6, of which waited for: 6 -> 6; matrix products, arithmetic and copies ran while one was open for 2% -> 0% of each run, Pallas kernels for 0% -> 0%
where the time goes in v2:
time: 758 us; the launch traced here: 753 us
  waiting for transfers between devices  445 us (59%)
  other arithmetic  209 us (28%)
  matrix products  51.4 us (7%)
  local copies, waits for them, and re-layouts  30.7 us (4%)
  between operations  14.7 us (2%)
    psum x6, waiting for transfers between devices, from_root(): return lax.psum(block, axis)  445 us
    another operation x24, other arithmetic, factor_block(): lower = jnp.linalg.cholesky(block)  100 us
    another operation x16, other arithmetic, factor_block(): lax.linalg.triangular_solve(lower, eye, left_side=True, lower=True)  84.9 us
    dot_general x2, matrix products, apply_update(): jnp.einsum('arb,csb->arcs', row_panel, col_panel, precision=lax.Precision...  28 us
    dot_general x26, matrix products, mm(): return jnp.matmul(a, b, precision=HIGH)  21.2 us
  transfers between devices with their start and end apart: 6, of which 6 were waited for; matrix products, arithmetic and copies ran while one was open for 0% of the time, Pallas kernels for 0%

profile of v2, /device:TPU:25, one launch (start us, length us, event | category | flops | bytes accessed | tf_op | source)
XLA Modules:
  0.0 752.7 jit_solution(4689376273525011006)
XLA Ops:
  6.6 0.8 and_and_fusion
  7.3 6.1 bitcast_select_fusion
  13.5 3.4 copy-done
  16.9 1.1 fusion.18
  18.4 56.3 %all-reduce.21.cloned.1.call-done = f32[512,512]{1,0:T(8,128)} async-done(((f32[512,512]{1,0:T(8,128)}), f32[512,512]{1,0:T(8,128)}) %all-reduce.21.cloned.1.call-update) | async-done | bytes 1048592 | tf_op jit(solution)/shard_map/psum | solution.py:11
  74.7 1.6 copy.37
  76.7 11.7 %cholesky.134 = f32[128,128]{1,0:T(8,128)S(1)} custom-call(f32[128,128]{1,0:T(8,128)S(1)} %fusion.93), custom_call_target="Cholesky" | custom-call | tf_op jit(solution)/shard_map/jit(cholesky)/cholesky | solution.py:19
  88.5 0.7 compare_reduce_fusion.7
  89.2 0.7 select_bitcast_fusion.11
  89.9 9.8 %custom-call.12 = f32[1,128,128]{1,2,0:T(8,128)S(1)} custom-call(f32[1,128,128]{2,1,0:T(8,128)S(1)} %get-tuple-element.27), custom_call_target="InvertDiagBlocksLowerTriangular" | custom-call | tf_op jit(solution)/shard_map/triangular_solve/custom-call.0 | solution.py:21
  100.9 11.7 %cholesky.145 = f32[128,128]{1,0:T(8,128)S(1)} custom-call(f32[128,128]{1,0:T(8,128)S(1)} %fusion.91), custom_call_target="Cholesky" | custom-call | tf_op jit(solution)/shard_map/jit(cholesky)/cholesky | solution.py:19
  112.7 0.7 compare_reduce_fusion.6
  113.4 0.7 select_bitcast_fusion.10
  114.1 10.3 %custom-call.13 = f32[1,128,128]{1,2,0:T(8,128)S(1)} custom-call(f32[1,128,128]{2,1,0:T(8,128)S(1)} %get-tuple-element.25), custom_call_target="InvertDiagBlocksLowerTriangular" | custom-call | tf_op jit(solution)/shard_map/triangular_solve/custom-call.0 | solution.py:21
  125.5 0.6 convolution_subtract_fusion.1
  126.2 11.7 %cholesky.156 = f32[128,128]{1,0:T(8,128)S(1)} custom-call(f32[128,128]{1,0:T(8,128)S(1)} %fusion.89), custom_call_target="Cholesky" | custom-call | tf_op jit(solution)/shard_map/jit(cholesky)/cholesky | solution.py:19
  138.0 0.7 compare_reduce_fusion.5
  138.7 0.7 select_bitcast_fusion.9
  139.4 9.8 %custom-call.14 = f32[1,128,128]{1,2,0:T(8,128)S(1)} custom-call(f32[1,128,128]{2,1,0:T(8,128)S(1)} %get-tuple-element.23), custom_call_target="InvertDiagBlocksLowerTriangular" | custom-call | tf_op jit(solution)/shard_map/triangular_solve/custom-call.0 | solution.py:21
  150.3 0.6 fusion.103
  151.4 11.9 %cholesky.167 = f32[128,128]{1,0:T(8,128)S(1)} custom-call(f32[128,128]{1,0:T(8,128)S(1)} %fusion.87), custom_call_target="Cholesky" | custom-call | tf_op jit(solution)/shard_map/jit(cholesky)/cholesky | solution.py:19
  163.3 0.7 compare_reduce_fusion.4
  164.0 0.7 select_bitcast_fusion.8
  164.7 9.8 %custom-call.15 = f32[1,128,128]{1,2,0:T(8,128)S(1)} custom-call(f32[1,128,128]{2,1,0:T(8,128)S(1)} %get-tuple-element.21), custom_call_target="InvertDiagBlocksLowerTriangular" | custom-call | tf_op jit(solution)/shard_map/triangular_solve/custom-call.0 | solution.py:21
  175.7 6.5 select_select_fusion.1
  182.3 85.0 %all-reduce.23.cloned.1.call-done = f32[2,512,512]{2,1,0:T(8,128)} async-done(((f32[2,512,512]{2,1,0:T(8,128)}), f32[2,512,512]{2,1,0:T(8,128)}) %all-reduce.23.cloned.1.call-update) | async-done | bytes 2097168 | tf_op jit(solution)/shard_map/psum | solution.py:11
  267.3 4.3 select_bitcast_fusion.3
  271.7 0.4 all-reduce.25.cloned.1.call-start
  272.2 81.4 %all-reduce.31.cloned.1.call-done = (f32[2,1,512,512]{3,2,0,1:T(8,128)}, f32[2,1,512,512]{3,2,0,1:T(8,128)}) async-done(((f32[2,1,512,512]{3,2,0,1:T(8,128)}, f32[2,1,512,512]{3,2,0,1:T(8,128)}), (f32[2,1,512,512]{3,2,0,1:T(8,128)}, f32[2,1,512,512]{3,2,0,1:T(8,128)})) %all-reduce.31.cloned.1.call-update) | async-done | bytes 4194320 | tf_op jit(solution)/shard_map/psum | solution.py:11
  353.7 2.8 pad_maximum_fusion
  357.1 1.7 slice-done.1
  358.9 0.6 copy-done.2
  359.4 14.0 %fusion = f32[2,512,4,512]{3,1,2,0:T(8,128)S(1)} fusion(f32[2,512,4,512]{3,1,2,0:T(8,128)S(1)} %bitcast.174, f32[2,512,512]{2,1,0:T(8,128)S(1)} %copy-done.2, pred[4]{0:T(512)(128)(4,1)S(1)} %get-tuple-element.36, pred[2,4]{1,0:T(4,128)(4,1)S(1)} %bitcast.179, f32[4,512,512,1]{2,1,0,3:T(8,128)S(1)} %bitcast.177), kind=kOutput, calls=%fused_computation.2 | convolution fusion | flops 12891193344 | bytes 23068684 | tf_op jit(solution)/shard_map/arb,csb->arcs/dot_general | solution.py:82
  373.4 3.4 copy-done.1
  376.8 1.1 fusion.12
  378.0 55.8 %all-reduce.25.cloned.1.call-done = f32[512,512]{1,0:T(8,128)} async-done(((f32[512,512]{1,0:T(8,128)}), f32[512,512]{1,0:T(8,128)}) %all-reduce.25.cloned.1.call-update) | async-done | bytes 1048592 | tf_op jit(solution)/shard_map/psum | solution.py:11
  433.8 1.6 copy.53
  436.3 11.7 %cholesky.178 = f32[128,128]{1,0:T(8,128)S(1)} custom-call(f32[128,128]{1,0:T(8,128)S(1)} %fusion.85), custom_call_target="Cholesky" | custom-call | tf_op jit(solution)/shard_map/jit(cholesky)/cholesky | solution.py:19
  448.0 0.7 compare_reduce_fusion.3
  448.7 0.7 select_bitcast_fusion.7
  449.5 9.8 %custom-call.16 = f32[1,128,128]{1,2,0:T(8,128)S(1)} custom-call(f32[1,128,128]{2,1,0:T(8,128)S(1)} %get-tuple-element.19), custom_call_target="InvertDiagBlocksLowerTriangular" | custom-call | tf_op jit(solution)/shard_map/triangular_solve/custom-call.0 | solution.py:21
  460.5 11.7 %cholesky.189 = f32[128,128]{1,0:T(8,128)S(1)} custom-call(f32[128,128]{1,0:T(8,128)S(1)} %fusion.83), custom_call_target="Cholesky" | custom-call | tf_op jit(solution)/shard_map/jit(cholesky)/cholesky | solution.py:19
  472.2 0.7 compare_reduce_fusion.2
  472.9 0.7 select_bitcast_fusion.6
  473.7 10.1 %custom-call.17 = f32[1,128,128]{1,2,0:T(8,128)S(1)} custom-call(f32[1,128,128]{2,1,0:T(8,128)S(1)} %get-tuple-element.17), custom_call_target="InvertDiagBlocksLowerTriangular" | custom-call | tf_op jit(solution)/shard_map/triangular_solve/custom-call.0 | solution.py:21
  484.9 0.6 convolution_subtract_fusion
  485.6 11.7 %cholesky.200 = f32[128,128]{1,0:T(8,128)S(1)} custom-call(f32[128,128]{1,0:T(8,128)S(1)} %fusion.81), custom_call_target="Cholesky" | custom-call | tf_op jit(solution)/shard_map/jit(cholesky)/cholesky | solution.py:19
  497.4 0.7 compare_reduce_fusion.1
  498.1 0.7 select_bitcast_fusion.5
  498.8 9.8 %custom-call.18 = f32[1,128,128]{1,2,0:T(8,128)S(1)} custom-call(f32[1,128,128]{2,1,0:T(8,128)S(1)} %get-tuple-element.15), custom_call_target="InvertDiagBlocksLowerTriangular" | custom-call | tf_op jit(solution)/shard_map/triangular_solve/custom-call.0 | solution.py:21
  509.7 0.6 fusion.104
  510.8 11.9 %cholesky.211 = f32[128,128]{1,0:T(8,128)S(1)} custom-call(f32[128,128]{1,0:T(8,128)S(1)} %fusion.79), custom_call_target="Cholesky" | custom-call | tf_op jit(solution)/shard_map/jit(cholesky)/cholesky | solution.py:19
  522.7 0.7 compare_reduce_fusion
  523.4 0.7 select_bitcast_fusion.4
  524.1 9.8 %custom-call.19 = f32[1,128,128]{1,2,0:T(8,128)S(1)} custom-call(f32[1,128,128]{2,1,0:T(8,128)S(1)} %get-tuple-element.13), custom_call_target="InvertDiagBlocksLowerTriangular" | custom-call | tf_op jit(solution)/shard_map/triangular_solve/custom-call.0 | solution.py:21
  535.1 6.5 select_select_fusion
  541.9 84.8 %all-reduce.27.cloned.1.call-done = f32[2,512,512]{2,1,0:T(8,128)} async-done(((f32[2,512,512]{2,1,0:T(8,128)}), f32[2,512,512]{2,1,0:T(8,128)}) %all-reduce.27.cloned.1.call-update) | async-done | bytes 2097168 | tf_op jit(solution)/shard_map/psum | solution.py:11
  626.7 4.3 select_bitcast_fusion.1
  631.1 82.0 %all-reduce.29.cloned.1.call-done = (f32[2,1,512,512]{3,2,0,1:T(8,128)}, f32[2,1,512,512]{3,2,0,1:T(8,128)}) async-done(((f32[2,1,512,512]{3,2,0,1:T(8,128)}, f32[2,1,512,512]{3,2,0,1:T(8,128)}), (f32[2,1,512,512]{3,2,0,1:T(8,128)}, f32[2,1,512,512]{3,2,0,1:T(8,128)})) %all-reduce.29.cloned.1.call-update) | async-done | bytes 4194320 | tf_op jit(solution)/shard_map/psum | solution.py:11
  713.1 2.8 pad_maximum_fusion.1
  716.5 1.7 slice-done.3
  718.2 0.6 copy-done.3
  718.8 14.0 %fusion.2 = f32[2,1,512,4,1,512]{5,2,3,0,4,1:T(8,128)S(1)} fusion(f32[2,512,4,512]{3,1,2,0:T(8,128)S(1)} %bitcast.176, f32[2,512,512]{2,1,0:T(8,128)S(1)} %copy-done.3, pred[4]{0:T(512)(128)(4,1)S(1)} %broadcast_compare_fusion.7, pred[2,4]{1,0:T(4,128)(4,1)S(1)} %bitcast.180, f32[4,512,512,1]{2,1,0,3:T(8,128)S(1)} %bitcast.178), kind=kOutput, calls=%fused_computation.4 | convolution fusion | flops 12891193344 | bytes 23068684 | tf_op jit(solution)/shard_map/arb,csb->arcs/dot_general | solution.py:82
  732.9 12.7 %copy.70 = f32[2,1,512,4,1,512]{5,4,3,2,1,0:T(1,128)} copy(f32[2,1,512,4,1,512]{5,2,3,0,4,1:T(8,128)S(1)} %fusion.2) | data formatting | bytes 16777216 | tf_op jit(solution)/shard_map/reshape | solution.py:91
  (119 shorter events, 13.4 us)
Async XLA Ops:
  6.5 68.1 %all-reduce.21.cloned.1.call-start = ((), (), s32[]{:S(2)}) async-start(), calls=%async_computation | async-start | bytes 2097152 | tf_op jit(solution)/shard_map/psum | solution.py:11
  13.5 3.4 copy-start
  18.0 249.3 %all-reduce.23.cloned.1.call-start = ((), (), s32[]{:S(2)}) async-start(), calls=%async_computation.1 | async-start | bytes 4194304 | tf_op jit(solution)/shard_map/psum | solution.py:11
  74.7 1.7 copy-start.4
  182.3 171.4 %all-reduce.31.cloned.1.call-start = ((), (), s32[]{:S(2)}) async-start(), calls=%async_computation.5 | async-start | bytes 8388608 | tf_op jit(solution)/shard_map/psum | solution.py:11
  271.7 162.1 %all-reduce.25.cloned.1.call-start = ((), (), s32[]{:S(2)}) async-start(), calls=%async_computation.2 | async-start | bytes 2097152 | tf_op jit(solution)/shard_map/psum | solution.py:11
  353.7 3.4 slice-start
  356.5 2.3 slice-start.1
  356.5 2.9 copy-start.2
  373.4 3.4 copy-start.1
  378.0 248.7 %all-reduce.27.cloned.1.call-start = ((), (), s32[]{:S(2)}) async-start(), calls=%async_computation.3 | async-start | bytes 4194304 | tf_op jit(solution)/shard_map/psum | solution.py:11
  433.8 1.7 copy-start.5
  541.7 171.4 %all-reduce.29.cloned.1.call-start = ((), (), s32[]{:S(2)}) async-start(), calls=%async_computation.4 | async-start | bytes 8388608 | tf_op jit(solution)/shard_map/psum | solution.py:11
  713.1 3.4 slice-start.2
  715.9 2.3 slice-start.3
  715.9 2.9 copy-start.3
Sparse Core Ops, SparseCore 0:
  18.1 56.5 all-reduce.20
  182.4 84.8 all-reduce.22
  271.8 81.8 all-reduce.30
  378.1 55.6 all-reduce.24
  541.8 84.8 all-reduce.26
  631.2 81.8 all-reduce.28

commit v3 on v2

v3 whole, which is shorter than its diff:
```python
import jax
import jax.numpy as jnp
from jax import lax
from jax.sharding import PartitionSpec as P

HIGH = lax.Precision.HIGHEST


def from_root(block, axis, source):
    block = jnp.where(lax.axis_index(axis) == source, block, jnp.zeros_like(block))
    return lax.psum(block, axis)


def mm(a, b):
    return jnp.matmul(a, b, precision=HIGH)


def factor_block(block):
    lower = jnp.linalg.cholesky(block)
    eye = jnp.eye(block.shape[0], dtype=jnp.float32)
    return lower, lax.linalg.triangular_solve(lower, eye, left_side=True, lower=True)


def factor_and_inverse(block):
    width = block.shape[0]
    if width <= 128:
        return factor_block(block)
    half = width // 2
    l00, i00 = factor_and_inverse(block[:half, :half])
    l10 = mm(block[half:, :half], i00.T)
    l11, i11 = factor_and_inverse(block[half:, half:] - mm(l10, l10.T))
    i10 = -mm(i11, mm(l10, i00))
    zero = jnp.zeros((half, half), jnp.float32)
    return jnp.block([[l00, zero], [l10, l11]]), jnp.block([[i00, zero], [i10, i11]])


def shards(covariance, keep):
    row_count = lax.axis_size("row")
    col_count = lax.axis_size("col")
    row_here = lax.axis_index("row")
    col_here = lax.axis_index("col")
    tile_rows = covariance.shape[0]
    width = covariance.shape[2]
    tile_cols = covariance.shape[3]
    group = row_count // col_count
    tiles = covariance.reshape(tile_rows, width, tile_cols, width)
    row_ids = jnp.arange(tile_rows) * row_count + row_here
    col_ids = jnp.arange(tile_cols) * col_count + col_here
    live = (keep.reshape(tile_rows, tile_cols) > 0) & (row_ids[:, None] >= col_ids[None, :])
    tiles = jnp.where(live[:, None, :, None], tiles, jnp.float32(0.0))

    def column_tiles(block):
        received = []
        for member in range(group):
            received.append(from_root(block, "row", col_here + member * col_count))
        stacked = jnp.stack(received, 1)
        return stacked.reshape(tile_rows * group, width, width)

    def symmetric(block):
        return (block + block.T) * 0.5

    marks = jnp.broadcast_to(live[:, 0, None, None].astype(jnp.float32), (tile_rows, 8, width))
    own = jnp.concatenate([tiles[:, :, 0, :], marks], 1)
    spread = lax.all_gather(own, "col")
    first_tiles = spread[0, :, :width]
    second_tiles = spread[1, :, :width]
    second_live = spread[1, :, width, :1]
    ids = row_ids[:, None, None]
    zero = jnp.float32(0.0)

    diag_tile = from_root(first_tiles[0], "row", 0)
    factor, inverse = factor_and_inverse(symmetric(diag_tile))
    row_one = jnp.where(ids > 0, mm(first_tiles, inverse.T), zero)

    local = row_one[0]
    pair = jnp.stack([local, second_tiles[0] - mm(local, local.T)])
    pair = from_root(pair, "row", 1)
    pair, later_one = lax.optimization_barrier((pair, row_one))
    col_one = column_tiles(later_one)
    below = pair[0]
    second_factor, second_inverse = factor_and_inverse(symmetric(pair[1]))
    reduced = second_tiles - mm(row_one, below.T) * second_live[:, :, None]
    row_two = jnp.where(ids > 1, mm(reduced, second_inverse.T), zero)
    later_two, col_one = lax.optimization_barrier((row_two, col_one))
    col_two = column_tiles(later_two)

    active = live[:, None, :, None]
    col_one = jnp.where(col_ids[:, None, None] > 0, col_one, zero)
    col_two = jnp.where(col_ids[:, None, None] > 1, col_two, zero)
    product = jnp.einsum("arb,csb->arcs", row_one, col_one, precision=HIGH)
    tiles = jnp.where(active, tiles - product, zero)
    product = jnp.einsum("arb,csb->arcs", row_two, col_two, precision=HIGH)
    tiles = jnp.where(active, tiles - product, zero)
    done_one = jnp.where(ids == 0, factor[None], row_one)
    done_two = jnp.where(ids == 1, second_factor[None], row_two)
    column = jnp.where(col_here == 0, done_one, done_two)
    tiles = jnp.where((col_ids < 2)[None, None, :, None], column[:, :, None, :], tiles)
    return tiles.reshape(tile_rows, 1, width, tile_cols, 1, width)


def solution(mesh):
    placed = (P(None, "row", None, None, "col", None), P(None, "row", None, "col"))
    return jax.shard_map(
        shards,
        mesh=mesh,
        in_specs=placed,
        out_specs=P(None, "row", None, None, "col", None),
        check_vma=False,
    )
```

time: 758 us -> 745 us (0.983)
  waiting for transfers between devices: 445 us -> 390 us
  matrix products: 51.4 us -> 74.4 us
  other arithmetic: 209 us -> 225 us
    psum x6 -> x4, waiting for transfers between devices: 445 us -> 240 us  [from_root(): return lax.psum(block, axis)]
    all_gather x0 -> x1, waiting for transfers between devices: none -> 150 us  [shards(): spread = lax.all_gather(own, 'col')]
    dot_general x2, matrix products: 28 us -> 39.8 us  [the longest x1 22 us: shards(): product = jnp.einsum('arb,csb->arcs', row_two, col_two, precision=HIGH)]
    dot_general x26 -> x28, matrix products: 21.2 us -> 31.8 us  [mm(): return jnp.matmul(a, b, precision=HIGH)]
  transfers between devices with their start and end apart: 6 -> 5, of which waited for: 6 -> 5; matrix products, arithmetic and copies ran while one was open for 0% -> 5% of each run, Pallas kernels for 0% -> 0%
where the time goes in v3:
time: 745 us; the launch traced here: 739 us
  waiting for transfers between devices  390 us (52%)
  other arithmetic  225 us (30%)
  matrix products  74.4 us (10%)
  local copies, waits for them, and re-layouts  35.1 us (5%)
  between operations  14.2 us (2%)
    psum x4, waiting for transfers between devices, from_root(): return lax.psum(block, axis)  240 us
    all_gather x1, waiting for transfers between devices, shards(): spread = lax.all_gather(own, 'col')  150 us
    another operation x24, other arithmetic, factor_block(): lower = jnp.linalg.cholesky(block)  100 us
    another operation x16, other arithmetic, factor_block(): lax.linalg.triangular_solve(lower, eye, left_side=True, lower=True)  88.4 us
    dot_general x28, matrix products, mm(): return jnp.matmul(a, b, precision=HIGH)  31.8 us
    dot_general x1, matrix products, shards(): product = jnp.einsum('arb,csb->arcs', row_two, col_two, precision=HIGH)  22 us
    dot_general x1, matrix products, shards(): product = jnp.einsum('arb,csb->arcs', row_one, col_one, precision=HIGH)  17.8 us
  transfers between devices with their start and end apart: 5, of which 5 were waited for; matrix products, arithmetic and copies ran while one was open for 5% of the time, Pallas kernels for 0%

profile of v3, /device:TPU:25, one launch (start us, length us, event | category | flops | bytes accessed | tf_op | source)
XLA Modules:
  0.0 738.8 jit_solution(13592069848332557036)
XLA Ops:
  7.5 6.1 bitcast_select_fusion
  13.9 1.5 pad_maximum_fusion.2
  15.5 150.0 %all-gather.3.cloned.1.call-done = f32[8,520,512]{2,1,0:T(8,128)} async-done(((f32[2,520,512]{2,1,0:T(8,128)}), f32[8,520,512]{2,1,0:T(8,128)}) %all-gather.3.cloned.1.call-update) | async-done | bytes 8519696 | tf_op jit(solution)/shard_map/all_gather | solution.py:64
  165.5 2.3 fusion.32
  168.0 57.2 %all-reduce.19.cloned.1.call-done = f32[512,512]{1,0:T(8,128)} async-done(((f32[512,512]{1,0:T(8,128)}), f32[512,512]{1,0:T(8,128)}) %all-reduce.19.cloned.1.call-update) | async-done | bytes 1048592 | tf_op jit(solution)/shard_map/psum | solution.py:11
  225.3 1.6 copy.72
  227.3 11.7 %cholesky.134 = f32[128,128]{1,0:T(8,128)S(1)} custom-call(f32[128,128]{1,0:T(8,128)S(1)} %fusion.112), custom_call_target="Cholesky" | custom-call | tf_op jit(solution)/shard_map/jit(cholesky)/cholesky | solution.py:19
  240.4 9.8 %custom-call.12 = f32[1,128,128]{1,2,0:T(8,128)S(1)} custom-call(f32[1,128,128]{2,1,0:T(8,128)S(1)} %get-tuple-element.33), custom_call_target="InvertDiagBlocksLowerTriangular" | custom-call | tf_op jit(solution)/shard_map/triangular_solve/custom-call.0 | solution.py:21
  251.4 11.7 %cholesky.145 = f32[128,128]{1,0:T(8,128)S(1)} custom-call(f32[128,128]{1,0:T(8,128)S(1)} %fusion.110), custom_call_target="Cholesky" | custom-call | tf_op jit(solution)/shard_map/jit(cholesky)/cholesky | solution.py:19
  263.8 1.3 select_bitcast_fusion.11
  265.1 10.0 %custom-call.13 = f32[1,128,128]{1,2,0:T(8,128)S(1)} custom-call(f32[1,128,128]{2,1,0:T(8,128)S(1)} %get-tuple-element.31), custom_call_target="InvertDiagBlocksLowerTriangular" | custom-call | tf_op jit(solution)/shard_map/triangular_solve/custom-call.0 | solution.py:21
  276.8 11.7 %cholesky.156 = f32[128,128]{1,0:T(8,128)S(1)} custom-call(f32[128,128]{1,0:T(8,128)S(1)} %fusion.108), custom_call_target="Cholesky" | custom-call | tf_op jit(solution)/shard_map/jit(cholesky)/cholesky | solution.py:19
  289.2 1.3 select_bitcast_fusion.10
  290.5 9.8 %custom-call.14 = f32[1,128,128]{1,2,0:T(8,128)S(1)} custom-call(f32[1,128,128]{2,1,0:T(8,128)S(1)} %get-tuple-element.29), custom_call_target="InvertDiagBlocksLowerTriangular" | custom-call | tf_op jit(solution)/shard_map/triangular_solve/custom-call.0 | solution.py:21
  302.9 12.1 %cholesky.167 = f32[128,128]{1,0:T(8,128)S(1)} custom-call(f32[128,128]{1,0:T(8,128)S(1)} %fusion.106), custom_call_target="Cholesky" | custom-call | tf_op jit(solution)/shard_map/jit(cholesky)/cholesky | solution.py:19
  315.7 1.3 select_bitcast_fusion.9
  317.0 9.8 %custom-call.15 = f32[1,128,128]{1,2,0:T(8,128)S(1)} custom-call(f32[1,128,128]{2,1,0:T(8,128)S(1)} %get-tuple-element.27), custom_call_target="InvertDiagBlocksLowerTriangular" | custom-call | tf_op jit(solution)/shard_map/triangular_solve/custom-call.0 | solution.py:21
  327.9 5.1 fusion.16
  333.0 3.1 fusion.20
  336.2 1.6 maximum_select_fusion
  338.0 1.4 slice_reduce_fusion
  341.8 56.6 %all-reduce.21.cloned.1.call-done = f32[2,512,512]{2,1,0:T(8,128)} async-done(((f32[2,512,512]{2,1,0:T(8,128)}), f32[2,512,512]{2,1,0:T(8,128)}) %all-reduce.21.cloned.1.call-update) | async-done | bytes 2097168 | tf_op jit(solution)/shard_map/psum | solution.py:11
  398.4 2.3 slice_bitcast_fusion.7
  400.7 1.6 copy.88
  402.2 2.4 bitcast_add_fusion
  404.7 1.6 copy.89
  406.3 1.0 copy-done.3
  407.4 0.9 fusion.104
  408.3 11.7 %cholesky.178 = f32[128,128]{1,0:T(8,128)S(1)} custom-call(f32[128,128]{1,0:T(8,128)S(1)} %fusion.104), custom_call_target="Cholesky" | custom-call | tf_op jit(solution)/shard_map/jit(cholesky)/cholesky | solution.py:19
  420.7 1.3 select_bitcast_fusion.8
  422.0 9.8 %custom-call.16 = f32[1,128,128]{1,2,0:T(8,128)S(1)} custom-call(f32[1,128,128]{2,1,0:T(8,128)S(1)} %get-tuple-element.25), custom_call_target="InvertDiagBlocksLowerTriangular" | custom-call | tf_op jit(solution)/shard_map/triangular_solve/custom-call.0 | solution.py:21
  432.1 1.0 fusion.91
  433.2 1.1 convolution_subtract_fusion.4
  435.4 11.7 %cholesky.189 = f32[128,128]{1,0:T(8,128)S(1)} custom-call(f32[128,128]{1,0:T(8,128)S(1)} %fusion.102), custom_call_target="Cholesky" | custom-call | tf_op jit(solution)/shard_map/jit(cholesky)/cholesky | solution.py:19
  447.9 1.3 select_bitcast_fusion.7
  449.1 10.0 %custom-call.17 = f32[1,128,128]{1,2,0:T(8,128)S(1)} custom-call(f32[1,128,128]{2,1,0:T(8,128)S(1)} %get-tuple-element.23), custom_call_target="InvertDiagBlocksLowerTriangular" | custom-call | tf_op jit(solution)/shard_map/triangular_solve/custom-call.0 | solution.py:21
  460.4 1.2 fusion.59
  461.6 1.6 select_maximum_fusion.4
  465.5 11.7 %cholesky.200 = f32[128,128]{1,0:T(8,128)S(1)} custom-call(f32[128,128]{1,0:T(8,128)S(1)} %fusion.100), custom_call_target="Cholesky" | custom-call | tf_op jit(solution)/shard_map/jit(cholesky)/cholesky | solution.py:19
  477.9 1.2 select_bitcast_fusion.6
  479.2 9.8 %custom-call.18 = f32[1,128,128]{1,2,0:T(8,128)S(1)} custom-call(f32[1,128,128]{2,1,0:T(8,128)S(1)} %get-tuple-element.21), custom_call_target="InvertDiagBlocksLowerTriangular" | custom-call | tf_op jit(solution)/shard_map/triangular_solve/custom-call.0 | solution.py:21
  489.3 1.0 fusion.89
  490.3 1.1 convolution_subtract_fusion.3
  491.6 12.1 %cholesky.211 = f32[128,128]{1,0:T(8,128)S(1)} custom-call(f32[128,128]{1,0:T(8,128)S(1)} %fusion.98), custom_call_target="Cholesky" | custom-call | tf_op jit(solution)/shard_map/jit(cholesky)/cholesky | solution.py:19
  504.3 1.3 select_bitcast_fusion.5
  505.6 9.8 %custom-call.19 = f32[1,128,128]{1,2,0:T(8,128)S(1)} custom-call(f32[1,128,128]{2,1,0:T(8,128)S(1)} %get-tuple-element.19), custom_call_target="InvertDiagBlocksLowerTriangular" | custom-call | tf_op jit(solution)/shard_map/triangular_solve/custom-call.0 | solution.py:21
  515.4 0.9 fusion.73
  516.3 2.7 select_bitcast_fusion.4
  522.3 1.6 copy.103
  523.9 1.4 fusion.25
  527.0 3.5 fusion.47
  530.5 7.7 %select_select_fusion = (f32[2,512,512]{2,1,0:T(8,128)}, f32[2,512,512]{2,1,0:T(8,128)}) fusion(f32[2,512,512]{2,1,0:T(8,128)S(1)} %fusion.16, f32[512,512]{1,0:T(8,128)S(1)} %get-tuple-element.47, f32[512,512]{1,0:T(8,128)S(1)} %get-tuple-element.48, pred[2]{0:T(512)(128)(4,1)S(1)} %get-tuple-element.46, pred[2]{0:T(512)(128)(4,1)S(1)} %broadcast_compare_fusion.6, ...), kind=kOutput, calls=%fused_computation.25 | convolution fusion | flops 3225944064 | bytes 13369359 | tf_op jit(solution)/shard_map/dot_general | solution.py:15
  538.2 62.4 %all-reduce.25.cloned.1.call-done = (f32[2,1,512,512]{3,2,0,1:T(8,128)}, f32[2,1,512,512]{3,2,0,1:T(8,128)}) async-done(((f32[2,1,512,512]{3,2,0,1:T(8,128)}, f32[2,1,512,512]{3,2,0,1:T(8,128)}), (f32[2,1,512,512]{3,2,0,1:T(8,128)}, f32[2,1,512,512]{3,2,0,1:T(8,128)})) %all-reduce.25.cloned.1.call-update) | async-done | bytes 4194320 | tf_op jit(solution)/shard_map/psum | solution.py:11
  600.6 2.7 pad_maximum_fusion
  603.3 2.5 copy.105
  605.8 2.7 select_bitcast_fusion.2
  608.6 17.8 %fusion.2 = f32[2,512,4,512]{3,1,2,0:T(8,128)} fusion(f32[4,512,512]{2,1,0:T(8,128)} %bitcast.203, f32[2,512,512]{2,1,0:T(8,128)S(1)} %fusion.16, pred[4]{0:T(512)(128)(4,1)S(1)} %get-tuple-element.44), kind=kOutput, calls=%fused_computation.7 | convolution fusion | flops 12885950464 | bytes 14680068 | tf_op jit(solution)/shard_map/arb,csb->arcs/dot_general | solution.py:90
  626.4 63.6 %all-reduce.23.cloned.1.call-done = (f32[2,1,512,512]{3,2,0,1:T(8,128)}, f32[2,1,512,512]{3,2,0,1:T(8,128)}) async-done(((f32[2,1,512,512]{3,2,0,1:T(8,128)}, f32[2,1,512,512]{3,2,0,1:T(8,128)}), (f32[2,1,512,512]{3,2,0,1:T(8,128)}, f32[2,1,512,512]{3,2,0,1:T(8,128)})) %all-reduce.23.cloned.1.call-update) | async-done | bytes 4194320 | tf_op jit(solution)/shard_map/psum | solution.py:11
  690.0 2.8 pad_maximum_fusion.1
  693.3 2.9 bitcast_select_fusion.1
  696.2 1.6 slice-done.3
  697.9 1.2 slice-done.1
  699.0 22.0 %select_bitcast_fusion = f32[2,1,512,4,1,512]{5,2,3,0,4,1:T(8,128)} fusion(f32[2,512,4,512]{3,1,2,0:T(8,128)S(1)} %bitcast.202, f32[2,512,512]{2,1,0:T(8,128)} %get-tuple-element.41, pred[4]{0:T(512)(128)(4,1)S(1)} %broadcast_compare_fusion.7, pred[2,4]{1,0:T(4,128)(4,1)S(1)} %bitcast.210, f32[4,512,512]{2,1,0:T(8,128)} %bitcast_select_fusion.1, ...), kind=kOutput, calls=%fused_computation.1 | convolution fusion | flops 12897484800 | bytes 33554444 | tf_op jit(solution)/shard_map/arb,csb->arcs/dot_general | solution.py:92
  721.1 11.0 %copy.107 = f32[2,1,512,4,1,512]{5,4,3,2,1,0:T(1,128)} copy(f32[2,1,512,4,1,512]{5,2,3,0,4,1:T(8,128)} %select_bitcast_fusion) | data formatting | bytes 16777216 | tf_op jit(solution)/shard_map/reshape | solution.py:98
  (142 shorter events, 28.0 us)
Async XLA Ops:
  6.5 159.0 %all-gather.3.cloned.1.call-start = ((), (), s32[]{:S(2)}) async-start(), calls=%async_computation.2 | async-start | bytes 10649600 | tf_op jit(solution)/shard_map/all_gather | solution.py:64
  15.4 209.9 %all-reduce.19.cloned.1.call-start = ((), (), s32[]{:S(2)}) async-start(), calls=%async_computation | async-start | bytes 2097152 | tf_op jit(solution)/shard_map/psum | solution.py:11
  167.8 230.6 %all-reduce.21.cloned.1.call-start = ((), (), s32[]{:S(2)}) async-start(), calls=%async_computation.1 | async-start | bytes 4194304 | tf_op jit(solution)/shard_map/psum | solution.py:11
  225.3 1.7 copy-start.2
  337.8 3.3 copy-start.12
  337.8 262.8 %all-reduce.25.cloned.1.call-start = ((), (), s32[]{:S(2)}) async-start(), calls=%async_computation.4 | async-start | bytes 8388608 | tf_op jit(solution)/shard_map/psum | solution.py:11
  406.3 1.0 copy-start.3
  407.3 53.1 %copy-start.4 = (f32[512,512]{0,1:T(8,128)S(1)}, f32[512,512]{0,1:T(8,128)}, u32[]{:S(2)}) copy-start(f32[512,512]{0,1:T(8,128)} %copy-done.3) | copy-start | bytes 3145732
  463.8 0.7 copy-start.8
  519.0 0.8 copy-start.13
  519.0 0.9 copy-start.14
  519.0 4.9 copy-start.5
  519.0 4.9 copy-start.7
  519.1 170.9 %all-reduce.23.cloned.1.call-start = ((), (), s32[]{:S(2)}) async-start(), calls=%async_computation.3 | async-start | bytes 8388608 | tf_op jit(solution)/shard_map/psum | solution.py:11
  523.9 1.8 copy-start.11
  523.9 2.1 copy-start.9
  523.9 2.7 copy-start.10
  523.9 3.1 copy-start.1
  527.0 3.5 copy-start.6
  527.0 3.5 copy-start.15
  603.3 2.5 copy-start
  690.0 6.3 slice-start.2
  692.8 3.4 slice-start
  692.8 5.0 slice-start.3
  693.3 5.7 slice-start.1
Sparse Core Ops, SparseCore 0:
  15.5 149.9 all-gather.2
  168.7 56.5 all-reduce.18
  337.9 60.4 all-reduce.20
  519.2 81.3 all-reduce.24
  608.7 81.2 all-reduce.22
